TPU v7x, 128 devices: a whole 4x4x4 slice. The times are simulated.
128 devices in a mesh: slab: 4 (over x_hi, core), sx: 4 (over z), syz: 8 (over x_lo, y).
Axes of the slice: x: 4 (x_hi: 2, x_lo: 2; x = x_hi * 2 + x_lo), y: 4, z: 4, core: 2. Of those that a mesh axis runs over, the one named last changes fastest.
Arguments:
- gauge_links: float32 [4, 2, 3, 3, 8, 12, 1024], P(None, None, None, None, 'slab', 'sx', 'syz'), may hold values from -1 to 1, as said below
- langevin_noise: bfloat16 [2, 4, 8, 8, 12, 1024], P(None, None, None, 'slab', 'sx', 'syz'), may hold values from -4 to 4
- separations: int32 [4], replicated, may hold values from 1 to 3, as said below
Outputs:
- correlator: float32 [4, 12, 1024], P('slab', 'sx', 'syz')
Inputs may be any that keep to these rules, and one draw needn't show every extreme that they name: Each 3x3 complex matrix of real part gauge_links[mu, 0] and imaginary part gauge_links[mu, 1] is unitary. `separations`: separations from 1 to 3 sites; at least one equals 3.
All inputs are finite; a program needn't handle non-finite values.
Results may differ from a plain program's by a relative error of at most 0.0003.
Values sent between devices are 32-bit elements; how exact they have to be, the bound alone decides.
A program may use at most 64 MiB of HBM per device.

v0:
```python
from functools import partial

import jax
import jax.numpy as jnp
from jax import lax
from jax.experimental import pallas as pl
from jax.experimental.pallas import tpu as pltpu
from jax.sharding import PartitionSpec as P

SITES_ALONG_Z = 32
SWEEPS = 2

step_drift = 0.2
step_noise = 0.4
root_third = 0.5773502691896258

MESH = pl.DeviceIdType.MESH
VMEM_LIMIT = 60 * 1024 * 1024

OWN = slice(2, 5)
FIELDS = ((0, 0), (0, 1), (1, 1), (2, 1), (3, 1), (1, 0), (2, 0), (3, 0), (1, 2), (2, 2), (3, 2))
FIELD_OF = {field: index for index, field in enumerate(FIELDS)}
KICKS = ((0, 0, 0), (0, 0, 1), (0, 1, 1), (0, 2, 1), (0, 3, 1), (1, 0, 0), (1, 0, 1))
KICK_OF = {kick: index for index, kick in enumerate(KICKS)}
LINK, KICK = 7, 4


def size(entry):
    return LINK if len(entry) == 2 else KICK


def placed(*groups):
    places, x_end, y_end = {}, 0, 0
    for group in groups:
        members = group if isinstance(group[0], tuple) else (group,)
        for half, entry in enumerate(members):
            places[entry] = (x_end, y_end, half)
            x_end += size(entry)
        y_end += size(members[0])
    return places, (x_end, y_end)


FIRST_GROUPS = ((0, 0), (0, 0, 0), (2, 0), ((3, 0), (1, 0)), ((1, 1), (3, 1)), (2, 1))
FROZEN_GROUPS = ((2, 2), ((3, 2), (1, 2)))
SECOND_GROUPS = ((0, 1), ((0, 0, 1), (0, 1, 1)))
LATE_GROUPS = (((0, 2, 1), (0, 3, 1)), ((1, 0, 0), (1, 0, 1)))
FIRST, FIRST_PAIRS = placed(*FIRST_GROUPS)
SECOND, SECOND_PAIRS = placed(*FROZEN_GROUPS, *SECOND_GROUPS)
LATE, LATE_PAIRS = placed(*LATE_GROUPS)
TURN, TURN_PAIRS = placed((0, 0), (0, 1), (1, 1))
TURN2, TURN2_PAIRS = placed((1, 1), (2, 1), (3, 1))
FIRST_ROWS = {
    (0, 0): (2, 2, 1, 1, 1, 1),
    (0, 0, 0): (1, 1, 0, 0, 1, 1),
    (2, 0): (1, 1, 1, 0, 1, 1),
    (3, 0): (1, 1, 0, 0, 1, 1),
    (1, 0): (2, 1, 2, 2, 1, 1),
    (1, 1): (2, 2, 1, 1, 1, 1),
    (3, 1): (2, 2, 2, 2, 2, 2),
    (2, 1): (2, 2, 2, 2, 2, 2),
}
FROZEN_ROWS = {
    (2, 2): (1, 2, 1, 0, 2, 1),
    (3, 2): (1, 2, 0, 0, 1, 1),
    (1, 2): (2, 2, 2, 2, 1, 1),
}
SECOND_ROWS = {
    (0, 1): (2, 3, 1, 1, 2, 2),
    (0, 0, 1): (1, 2, 0, 0, 1, 1),
    (0, 1, 1): (2, 1, 2, 2, 1, 1),
}
LATE_ROWS = {
    (0, 2, 1): (1, 1, 1, 0, 1, 0),
    (0, 3, 1): (1, 1, 0, 0, 0, 0),
    (1, 0, 0): (1, 1, 0, 0, 0, 0),
    (1, 0, 1): (1, 1, 0, 0, 0, 0),
}
TURN_ROWS = {
    (0, 0): (2, 2, 2, 2, 2, 2),
    (0, 1): (2, 2, 2, 2, 2, 2),
    (1, 1): (2, 1, 2, 2, 1, 1),
}
TURN2_ROWS = {
    (1, 1): (2, 1, 1, 1, 0, 0),
    (2, 1): (1, 1, 1, 0, 1, 0),
    (3, 1): (2, 2, 1, 1, 1, 1),
}
FACES = tuple((dx, dy) for dx in (-1, 0, 1) for dy in (-1, 0, 1))
FACES = tuple(sorted(FACES, key=lambda face: -abs(face[0]) - abs(face[1])))
RING = tuple(face for face in FACES if face != (0, 0))


def runs(places, rows, face):
    dx, dy = face
    found = {}
    for entry, needed in rows.items():
        if dx == 0:
            count = 3
        elif dy == 0:
            count = needed[0 if dx == 1 else 1]
        else:
            count = needed[(2 if dx == 1 else 4) + (0 if dy == 1 else 1)]
        low = places[entry][0 if dy == 0 else 1]
        high = low + size(entry)
        found[low] = (high, max(count, found.get(low, (0, 0))[1]))
    merged = []
    for low, (high, count) in sorted(found.items()):
        if not count:
            continue
        if merged and merged[-1][1:] == (low, count):
            merged[-1] = (merged[-1][0], high, count)
        else:
            merged.append((low, high, count))
    return merged


def count_of(places, rows, faces):
    return sum(len(runs(places, rows, face)) for face in faces)


COPIES = (
    count_of(FIRST, FIRST_ROWS, RING)
    + 3
    + count_of(SECOND, FROZEN_ROWS, RING)
    + count_of(SECOND, SECOND_ROWS, RING)
    + count_of(LATE, LATE_ROWS, RING)
    + sum(count_of(TURN, {entry: TURN_ROWS[entry]}, RING) for entry in TURN)
    + sum(count_of(TURN2, {entry: TURN2_ROWS[entry]}, RING) for entry in TURN2)
    + 7 * SWEEPS
)


def rows_sent(dx, count):
    if dx == 1:
        return pl.ds(5 - count, count), pl.ds(2 - count, count)
    if dx == -1:
        return pl.ds(2, count), pl.ds(5, count)
    return pl.ds(2, 3), pl.ds(2, 3)


def mm(a, b):
    real = imag = None
    for k in range(3):
        ar, ai = a[0][:, k][:, None], a[1][:, k][:, None]
        br, bi = b[0][k][None], b[1][k][None]
        re, im = ar * br - ai * bi, ar * bi + ai * br
        real, imag = (re, im) if real is None else (real + re, imag + im)
    return real, imag


def mm_nh(a, b):
    real = imag = None
    for k in range(3):
        ar, ai = a[0][:, k][:, None], a[1][:, k][:, None]
        br, bi = b[0][:, k][None], b[1][:, k][None]
        re, im = ar * br + ai * bi, ai * br - ar * bi
        real, imag = (re, im) if real is None else (real + re, imag + im)
    return real, imag


def mm_hn(a, b):
    real = imag = None
    for k in range(3):
        ar, ai = a[0][k][:, None], a[1][k][:, None]
        br, bi = b[0][k][None], b[1][k][None]
        re, im = ar * br + ai * bi, ar * bi - ai * br
        real, imag = (re, im) if real is None else (real + re, imag + im)
    return real, imag


def times(a, b):
    return a[0] * b[0] - a[1] * b[1], a[0] * b[1] + a[1] * b[0]


def conj_times(a, b):
    return a[0] * b[0] + a[1] * b[1], a[0] * b[1] - a[1] * b[0]


def add(a, b):
    return a[0] + b[0], a[1] + b[1]


def cross(re, im):
    entry = [(re[k], im[k]) for k in range(6)]
    found = []
    for j in range(3):
        k, m = (j + 1) % 3, (j + 2) % 3
        one, two = times(entry[k], entry[3 + m]), times(entry[m], entry[3 + k])
        found.append((one[0] - two[0], one[1] - two[1]))
    return found


def compress(re, im):
    terms = [times((re[6 + j], im[6 + j]), value) for j, value in enumerate(cross(re, im))]
    phase = add(add(terms[0], terms[1]), terms[2])
    return (
        jnp.concatenate([re[0:6], phase[0][None]], axis=0),
        jnp.concatenate([im[0:6], phase[1][None]], axis=0),
    )


def restore(re, im):
    third = [conj_times(value, (re[6], im[6])) for value in cross(re, im)]
    return (
        jnp.concatenate([re[0:6], jnp.stack([value[0] for value in third])], axis=0),
        jnp.concatenate([im[0:6], jnp.stack([value[1] for value in third])], axis=0),
    )


def rotated(product, noise, link):
    mr, mi = product
    n = noise
    drift = 0.25 * step_drift
    kick = 0.25 * step_noise

    def off(i, j, nr, ni):
        return (
            kick * nr - drift * (mr[i, j] - mr[j, i]),
            kick * ni - drift * (mi[i, j] + mi[j, i]),
        )

    p = off(0, 1, n[1], n[0])
    q = off(0, 2, n[4], n[3])
    r = off(1, 2, n[6], n[5])
    third = (mi[0, 0] + mi[1, 1] + mi[2, 2]) / 3.0
    eighth = root_third * n[7]
    a = kick * (eighth + n[2]) - 2.0 * drift * (mi[0, 0] - third)
    b = kick * (eighth - n[2]) - 2.0 * drift * (mi[1, 1] - third)
    c = -(a + b)
    pp = p[0] * p[0] + p[1] * p[1]
    qq = q[0] * q[0] + q[1] * q[1]
    rr = r[0] * r[0] + r[1] * r[1]
    bc, ac, ab = b * c, a * c, a * b
    pr = times(p, r)
    real = 1.0 + (pp + qq + rr) - (ab + ac + bc)
    odd = a * rr + b * qq + c * pp - a * bc - 2.0 * (pr[1] * q[0] - pr[0] * q[1])
    weight = 2.0 / (real * real + odd * odd)
    inv = (real * weight, odd * weight)
    rs = conj_times(r, q)
    ps = conj_times(p, q)
    s01 = (c * p[1] - rs[0], -c * p[0] - rs[1])
    s02 = (b * q[1] + pr[0], pr[1] - b * q[0])
    s12 = (a * r[1] - ps[0], -a * r[0] - ps[1])
    adj = [
        [(1.0 + rr - bc, a), add(s01, p), add(s02, q)],
        [(s01[0] - p[0], p[1] - s01[1]), (1.0 + qq - ac, b), add(s12, r)],
        [(s02[0] - q[0], q[1] - s02[1]), (s12[0] - r[0], r[1] - s12[1]), (1.0 + pp - ab, c)],
    ]
    rotation = [[times(entry, inv) for entry in row] for row in adj]
    for i in range(3):
        rotation[i][i] = (rotation[i][i][0] - 1.0, rotation[i][i][1])
    stacked = tuple(
        jnp.stack([jnp.stack([entry[part] for entry in row]) for row in rotation])
        for part in range(2)
    )
    return mm(stacked, link)


def kernel(
    links_hbm, kicks_hbm, separations_hbm, out, windows,
    links, kicks, separations, fetch_sem, first_set, second_set, late_set, turn_set, turn2_set,
    win, kwin, held, lines, send_sem, recv_sem,
):
    slabs, sxs, syzs = (lax.axis_size(axis) for axis in ("slab", "sx", "syz"))
    slab, sx, syz = (lax.axis_index(axis) for axis in ("slab", "sx", "syz"))

    def peer(ds, dx, dy):
        return (
            lax.rem(slab + ds + slabs, slabs),
            lax.rem(sx + dx + sxs, sxs),
            lax.rem(syz + dy + syzs, syzs),
        )

    peers = [(0, *face) for face in RING] + [(1, 0, 0)]
    barrier = pltpu.get_barrier_semaphore()
    for one in peers:
        pl.semaphore_signal(barrier, inc=1, device_id=peer(*one), device_id_type=MESH)

    fetches = [
        pltpu.make_async_copy(links_hbm, links, fetch_sem.at[0]),
        pltpu.make_async_copy(kicks_hbm, kicks, fetch_sem.at[1]),
        pltpu.make_async_copy(separations_hbm, separations, fetch_sem.at[2]),
    ]
    for fetch in fetches:
        fetch.start()
    started = []

    def send(src, dst, target):
        index = len(started)
        copy = pltpu.make_async_remote_copy(
            src_ref=src,
            dst_ref=dst,
            send_sem=send_sem.at[index],
            recv_sem=recv_sem.at[index],
            device_id=peer(*target),
            device_id_type=MESH,
        )
        copy.start()
        started.append(copy)
        return copy

    shape = (8, 128)
    lane = lax.broadcasted_iota(jnp.int32, shape, 1)
    row = lax.broadcasted_iota(jnp.int32, shape, 0)
    half = lane % 16
    quarter = lane // 32
    low_half = lane < 64
    middle = jnp.logical_and(lane >= 32, lane < 96)
    first_of_half = (lane % 64) < 32
    odd_site = (sx * 3 + row + lane // 16) % 2
    is_odd = [odd_site == 1, odd_site == 0]
    last_half, first_half = half == 15, half == 0

    def own_index(time):
        lane3 = lax.broadcasted_iota(jnp.int32, (3, 128), 1)
        row3 = lax.broadcasted_iota(jnp.int32, (3, 128), 0)
        y = (lane3 % 64) // 16
        bit = (time + sx * 3 + row3 + y + lane3 // 64) % 2
        return y * 32 + (lane3 % 16) * 2 + bit

    own_gather = [own_index(0), own_index(1)]

    first3 = first_of_half[0:3]
    second3 = (lane[0:3] % 32) >= 16

    def put(bufs, places, *entries):
        x_buf, p_buf, m_buf = bufs[:3]
        upper, lower = [], []
        for entry, first, second in entries:
            x, y, _ = places[entry]
            count = size(entry)
            rolled = pltpu.roll(first, 96, 2)
            x_buf[2 * x : 2 * x + count, OWN] = first
            x_buf[2 * x + count : 2 * x + 2 * count, OWN] = second
            upper.append(jnp.where(first3, rolled, second))
            lower.append(jnp.where(first3, second, rolled))
        if len(entries) == 2:
            upper = [jnp.where(second3, upper[0], pltpu.roll(upper[1], 112, 2))]
            lower = [jnp.where(second3, pltpu.roll(lower[1], 16, 2), lower[0])]
        p_buf[y : y + count, OWN] = upper[0]
        m_buf[y : y + count, OWN] = lower[0]

    def spread(bufs, places, rows):
        copies = []
        for face in RING:
            for low, high, count in runs(places, rows, face):
                dx, dy = face
                out_rows, in_rows = rows_sent(dx, count)
                if dy == 0:
                    src = dst = bufs[0]
                    low, high = 2 * low, 2 * high
                else:
                    src, dst = (bufs[1], bufs[3]) if dy == 1 else (bufs[2], bufs[4])
                copies.append(
                    send(
                        src.at[pl.ds(low, high - low), out_rows],
                        dst.at[pl.ds(low, high - low), in_rows],
                        (0, dx, dy),
                    )
                )
        return copies

    def assemble(bufs, place, count):
        x_buf, _, _, lo_buf, hi_buf = bufs
        x, y, second = place
        lo, hi = lo_buf[y : y + count], hi_buf[y : y + count]
        if second:
            lo, hi = pltpu.roll(lo, 16, 2), pltpu.roll(hi, 112, 2)
        found = [[None, None], [None, None]]
        for member in range(2):
            start = 2 * x + member * count
            own = x_buf[start : start + count]
            for parity in range(2):
                q = 2 * parity + member
                edge = jnp.where(quarter == q, lo, hi)
                if q:
                    edge = pltpu.roll(edge, 128 - 32 * q, 2)
                centre = pltpu.roll(own, 32 if parity == 0 else 96, 2)
                found[parity][member] = jnp.where(middle, centre, edge)
        return found

    def take_in(bufs, places, entries):
        for entry in entries:
            if len(entry) == 2:
                found = assemble(bufs, places[entry], LINK)
                for parity in range(2):
                    for part, value in enumerate(restore(*found[parity])):
                        win[FIELD_OF[entry], parity, part] = value
            else:
                found = assemble(bufs, places[entry], KICK)
                for parity in range(2):
                    for member in range(2):
                        kwin[KICK_OF[entry], parity, 4 * member : 4 * member + 4] = found[parity][member]

    def packed(parts, time):
        return jnp.stack([jnp.take_along_axis(part, own_gather[time], axis=1) for part in parts])

    def pack(bufs, places, groups):
        for group in groups:
            members = []
            for entry in group if isinstance(group[0], tuple) else (group,):
                if len(entry) == 2:
                    direction, time = entry
                    whole = [
                        packed(
                            [
                                links[direction, part, i, j, :, time]
                                for i in range(3)
                                for j in range(3)
                            ],
                            time,
                        )
                        for part in range(2)
                    ]
                    members.append((entry, *compress(*whole)))
                else:
                    sweep, direction, time = entry
                    parts = [
                        kicks[sweep, direction, a, :, time].astype(jnp.float32) for a in range(8)
                    ]
                    members.append((entry, packed(parts[:4], time), packed(parts[4:], time)))
            put(bufs, places, *members)

    def wait(copies):
        for copy in copies:
            copy.wait_recv()

    for fetch in fetches:
        fetch.wait()
    pack(first_set, FIRST, FIRST_GROUPS)
    pl.semaphore_wait(barrier, len(peers))

    frozen_copies = []
    for k in range(3):
        low, high = FIRST[2, 0][min(k, 1)], FIRST[1, 0][min(k, 1)] + LINK
        goal = SECOND[2, 2][min(k, 1)]
        if k == 0:
            low, high, goal = 2 * low, 2 * high, 2 * goal
        frozen_copies.append(
            send(
                first_set[k].at[pl.ds(low, high - low), pl.ds(2, 3)],
                second_set[k].at[pl.ds(goal, high - low), pl.ds(2, 3)],
                (-1, 0, 0),
            )
        )
    first_copies = spread(first_set, FIRST, FIRST_ROWS)
    pack(second_set, SECOND, SECOND_GROUPS)
    second_copies = spread(second_set, SECOND, SECOND_ROWS)
    pack(late_set, LATE, LATE_GROUPS)
    wait(frozen_copies)
    second_copies += spread(second_set, SECOND, FROZEN_ROWS)
    late_copies = spread(late_set, LATE, LATE_ROWS)

    def shifted(pair, axis, sign, time, parity):
        def one(value):
            if axis == 0:
                return value
            flat = value.reshape(9, 8, 128)
            if axis == 1:
                flat = pltpu.roll(flat, 7 if sign == 1 else 1, 1)
            elif axis == 2:
                flat = pltpu.roll(flat, 112 if sign == 1 else 16, 2)
            else:
                odd = is_odd[(time + parity) % 2]
                if sign == 1:
                    inner = jnp.where(last_half, pltpu.roll(flat, 15, 2), pltpu.roll(flat, 127, 2))
                    flat = jnp.where(odd, inner, flat)
                else:
                    inner = jnp.where(first_half, pltpu.roll(flat, 113, 2), pltpu.roll(flat, 1, 2))
                    flat = jnp.where(odd, flat, inner)
            return flat.reshape(3, 3, 8, 128)

        return one(pair[0]), one(pair[1])

    def link(direction, time, parity):
        field = FIELD_OF[direction, time]
        return tuple(win[field, parity, part].reshape(3, 3, 8, 128) for part in range(2))

    def staples(mu, time, parity, planes):
        total = None
        other = 1 - parity
        for nu in planes:
            if mu == 0:
                ahead = link(nu, time + 1, other)
                ahead_low = link(nu, time + 1, parity)
            else:
                ahead = shifted(link(nu, time, other), mu, 1, time, parity)
            if nu == 0:
                above, below = link(mu, time + 1, other), link(mu, time - 1, other)
                low_time = time - 1
            else:
                above = shifted(link(mu, time, other), nu, 1, time, parity)
                below = link(mu, time, other)
                low_time = time
            if mu != 0:
                ahead_low = shifted(
                    link(nu, low_time, parity), mu, 1, low_time, other
                )
            upper = mm_nh(mm_nh(ahead, above), link(nu, time, parity))
            lower = mm_hn(mm(below, ahead_low), link(nu, low_time, other))
            lower = shifted(lower, nu, -1, time, parity)
            both = add(upper, lower)
            total = both if total is None else add(total, both)
        return total

    def ahead_of(slot, mu, time, parity, planes):
        for part, value in enumerate(staples(mu, time, parity, planes)):
            held[slot, part] = value

    def substep(sweep, mu, parity, time=1, slot=None, done=()):
        current = link(mu, time, parity)
        noise = kwin[KICK_OF[sweep, mu, time], parity]
        planes = [nu for nu in range(4) if nu != mu and nu not in done]
        total = staples(mu, time, parity, planes)
        if done:
            total = add(total, (held[slot, 0], held[slot, 1]))
        new = rotated(mm(current, total), noise, current)
        field = FIELD_OF[mu, time]
        for part in range(2):
            win[field, parity, part] = new[part].reshape(9, 8, 128)

    def own_part(two):
        return jnp.where(low_half, pltpu.roll(two[0], 96, 2), pltpu.roll(two[1], 32, 2))

    def pass_on(bufs, places, rows, entry):
        whole = [
            own_part([win[FIELD_OF[entry], parity, part] for parity in range(2)])[:, OWN]
            for part in range(2)
        ]
        put(bufs, places, (entry, *compress(*whole)))
        return spread(bufs, places, {entry: rows[entry]})

    def measure(sweep):
        products = [mm(link(0, 0, parity), link(0, 1, 1 - parity)) for parity in range(2)]
        whole = [
            own_part([product[part].reshape(9, 8, 128) for product in products])[:, OWN]
            for part in range(2)
        ]
        for part, value in enumerate(compress(*whole)):
            lines[sweep, 0, LINK * part : LINK * part + LINK, 0:3] = value
    def hand_lines(sweep, slabs_below):
        copies = {}
        src = lines.at[sweep, 0, :, pl.ds(0, 3)]
        for ds in slabs_below:
            copies[ds, 1] = send(src, lines.at[sweep, ds, :, pl.ds(3, 3)], (-ds, -1, 0))
        for ds in slabs_below:
            if ds:
                copies[ds, 0] = send(src, lines.at[sweep, ds, :, pl.ds(0, 3)], (-ds, 0, 0))
        return copies

    wait(first_copies)
    take_in(first_set, FIRST, FIRST)
    substep(0, 0, 0, 0)
    substep(0, 0, 1, 0)
    turn_first = pass_on(turn_set, TURN, TURN_ROWS, (0, 0))
    ahead_of(1, 1, 1, 0, (2, 3))
    wait(second_copies)
    take_in(second_set, SECOND, SECOND)
    substep(0, 0, 0, 1)
    substep(0, 0, 1, 1)
    turn_first += pass_on(turn_set, TURN, TURN_ROWS, (0, 1))
    substep(0, 1, 0, 1, 1, (2, 3))
    turn_last = pass_on(turn_set, TURN, TURN_ROWS, (1, 1))
    measure(0)
    line_copies = hand_lines(0, (1, 3, 0))
    ahead_of(0, 2, 1, 0, (3,))
    wait(late_copies)
    take_in(late_set, LATE, LATE)
    wait(turn_first)
    take_in(turn_set, TURN, ((0, 0), (0, 1)))
    ahead_of(1, 1, 1, 1, (0,))
    ahead_of(2, 2, 1, 1, (0,))
    ahead_of(3, 3, 1, 0, (0,))
    wait(turn_last)
    take_in(turn_set, TURN, ((1, 1),))
    substep(0, 1, 1, 1, 1, (0,))
    turn_first = pass_on(turn2_set, TURN2, TURN2_ROWS, (1, 1))
    substep(0, 2, 0, 1, 0, (3,))
    substep(0, 2, 1, 1, 2, (0,))
    turn_first += pass_on(turn2_set, TURN2, TURN2_ROWS, (2, 1))
    substep(0, 3, 0, 1, 3, (0,))
    turn_last = pass_on(turn2_set, TURN2, TURN2_ROWS, (3, 1))
    ahead_of(0, 3, 1, 1, (0,))
    wait([line_copies.pop((3, 0))])
    line_copies.update(hand_lines(0, (2,)))
    wait(turn_first)
    take_in(turn2_set, TURN2, ((1, 1), (2, 1)))
    ahead_of(1, 0, 0, 0, (1, 2))
    ahead_of(2, 0, 1, 0, (1, 2))
    wait(turn_last)
    take_in(turn2_set, TURN2, ((3, 1),))
    substep(0, 3, 1, 1, 0, (0,))
    for time in range(2):
        substep(1, 0, 0, time, 1 + time, (1, 2))
        substep(1, 0, 1, time)
    measure(1)
    last_copies = hand_lines(1, (2, 1, 3, 0))
    keep = pltpu.make_async_copy(win, windows, fetch_sem.at[3])
    keep.start()

    def line(sweep, ds):
        whole = restore(lines[sweep, ds, 0:LINK], lines[sweep, ds, LINK : 2 * LINK])
        return tuple(part.reshape(3, 3, 8, 128) for part in whole)

    wait(line_copies.values())
    line_of = [[line(0, ds) for ds in range(4)]]
    low, high = {(0, 0): mm(line_of[0][0], line_of[0][1])}, {(0, 0): mm(line_of[0][2], line_of[0][3])}
    wait(last_copies.values())
    line_of.append([line(1, ds) for ds in range(4)])
    for pick in ((0, 1), (1, 0), (1, 1)):
        low[pick] = mm(line_of[pick[0]][0], line_of[pick[1]][1])
        high[pick] = mm(line_of[pick[0]][2], line_of[pick[1]][3])
    loops = []
    for left in low.values():
        for right in high.values():
            rr, ri = (jnp.swapaxes(part, 0, 1) for part in right)
            loops.append(jnp.sum((left[0] * rr - left[1] * ri).reshape(9, 8, 128), axis=0))
            loops.append(jnp.sum((left[0] * ri + left[1] * rr).reshape(9, 8, 128), axis=0))
    loops = jnp.stack(loops)
    distance = separations[slab]
    result = None
    for r in (3, 2, 1):
        far = pltpu.roll(loops, 8 - r, 1)
        if r % 2:
            far = pltpu.roll(far, 64, 2)
        value = jnp.sum(loops * far, axis=0)
        result = value if result is None else jnp.where(distance == r, value, result)
    lane3 = lax.broadcasted_iota(jnp.int32, (3, 128), 1)
    row3 = lax.broadcasted_iota(jnp.int32, (3, 128), 0)
    y, z = lane3 // 32, lane3 % 32
    index = ((z + y + row3 + sx * 3) % 2) * 64 + y * 16 + z // 2
    out[:, 0] = jnp.take_along_axis(result[0:3], index, axis=1)

    keep.wait()
    for copy in started:
        copy.wait_send()


def extended_2(block, sides, width):
    for axis, dim in sides:
        count = lax.axis_size(axis)
        forward = [(i, i + 1) for i in range(count - 1)]
        forward.append((count - 1, 0))
        backward = [(target, source) for source, target in forward]
        low = lax.ppermute(
            lax.slice_in_dim(block, block.shape[dim] - width, None, axis=dim), axis, forward
        )
        high = lax.ppermute(lax.slice_in_dim(block, 0, width, axis=dim), axis, backward)
        block = jnp.concatenate([low, block, high], axis=dim)
    return block


def shifted(block, axis, distance):
    devices = range(lax.axis_size(axis))
    route = [((i - distance) % len(devices), i) for i in devices]
    return lax.ppermute(block, axis, route)


def swapped(matrix_part):
    return jnp.swapaxes(matrix_part, 0, 1)


def dagger(matrix):
    return jnp.stack([swapped(matrix[0]), -swapped(matrix[1])])


def matrix_product(first, second):
    summed = None
    for middle in range(first.shape[1]):
        first_real = first[0][:, middle][:, None]
        first_imag = first[1][:, middle][:, None]
        second_real = second[0][middle][None]
        second_imag = second[1][middle][None]
        term_value = jnp.stack(
            [
                first_real * second_real - first_imag * second_imag,
                first_real * second_imag + first_imag * second_real,
            ]
        )
        summed = term_value if summed is None else summed + term_value
    return summed


def identity_like(matrix_part):
    return jnp.eye(3, dtype=matrix_part.dtype).reshape((3, 3) + (1,) * (matrix_part.ndim - 2))


def traceless_anti(matrix):
    anti_real = 0.5 * (matrix[0] - swapped(matrix[0]))
    anti_imag = 0.5 * (matrix[1] + swapped(matrix[1]))
    trace_third = (anti_imag[0, 0] + anti_imag[1, 1] + anti_imag[2, 2]) / 3.0
    anti_imag = anti_imag - identity_like(anti_imag) * trace_third[None, None]
    return jnp.stack([anti_real, anti_imag])


def algebra(coeffs):
    zero_part = jnp.zeros_like(coeffs[0])
    diag_first = coeffs[2] + root_third * coeffs[7]
    diag_second = -coeffs[2] + root_third * coeffs[7]
    diag_third = -2.0 * root_third * coeffs[7]
    herm_real = jnp.stack(
        [
            jnp.stack([diag_first, coeffs[0], coeffs[3]]),
            jnp.stack([coeffs[0], diag_second, coeffs[5]]),
            jnp.stack([coeffs[3], coeffs[5], diag_third]),
        ]
    )
    herm_imag = jnp.stack(
        [
            jnp.stack([zero_part, -coeffs[1], -coeffs[4]]),
            jnp.stack([coeffs[1], zero_part, -coeffs[6]]),
            jnp.stack([coeffs[4], coeffs[6], zero_part]),
        ]
    )
    return 0.5 * jnp.stack([-herm_imag, herm_real])


def complex_times(first, second):
    return (
        first[0] * second[0] - first[1] * second[1],
        first[0] * second[1] + first[1] * second[0],
    )


def cayley(generator, matrix):
    shift_real = identity_like(generator[0]) - 0.5 * generator[0]
    shift_imag = -0.5 * generator[1]

    def element(row_index, col_index):
        return (shift_real[row_index % 3, col_index % 3], shift_imag[row_index % 3, col_index % 3])

    cofactor = []
    for row_index in range(3):
        cof_row = []
        for col_index in range(3):
            forward = complex_times(
                element(row_index + 1, col_index + 1), element(row_index + 2, col_index + 2)
            )
            backward = complex_times(
                element(row_index + 1, col_index + 2), element(row_index + 2, col_index + 1)
            )
            cof_row.append((forward[0] - backward[0], forward[1] - backward[1]))
        cofactor.append(cof_row)
    det_real = 0.0
    det_imag = 0.0
    for col_index in range(3):
        det_term = complex_times(element(0, col_index), cofactor[0][col_index])
        det_real = det_real + det_term[0]
        det_imag = det_imag + det_term[1]
    weight = 1.0 / (det_real * det_real + det_imag * det_imag)
    inverse_det = (det_real * weight, -det_imag * weight)
    rotation_real = []
    rotation_imag = []
    for row_index in range(3):
        real_row = []
        imag_row = []
        for col_index in range(3):
            inverse_entry = complex_times(cofactor[col_index][row_index], inverse_det)
            delta_value = 1.0 if row_index == col_index else 0.0
            real_row.append(2.0 * inverse_entry[0] - delta_value)
            imag_row.append(2.0 * inverse_entry[1])
        rotation_real.append(jnp.stack(real_row))
        rotation_imag.append(jnp.stack(imag_row))
    rotation = jnp.stack([jnp.stack(rotation_real), jnp.stack(rotation_imag)])
    return matrix_product(rotation, matrix)


def unit_step(direction):
    return tuple((1 if axis_number == direction else 0 for axis_number in range(4)))


def add_steps(first, second):
    return tuple((first_part + second_part for first_part, second_part in zip(first, second)))


def negate(offsets):
    return tuple((-part_value for part_value in offsets))


def staple_sum(fetcher, direction):
    summed = None
    resting = (0, 0, 0, 0)
    onward = unit_step(direction)
    for transverse in range(4):
        if transverse == direction:
            continue
        across = unit_step(transverse)
        upper_loop = matrix_product(
            matrix_product(fetcher(transverse, onward), dagger(fetcher(direction, across))),
            dagger(fetcher(transverse, resting)),
        )
        lower_loop = matrix_product(
            matrix_product(
                dagger(fetcher(transverse, add_steps(onward, negate(across)))),
                dagger(fetcher(direction, negate(across))),
            ),
            fetcher(transverse, negate(across)),
        )
        summed = upper_loop + lower_loop if summed is None else summed + upper_loop + lower_loop
    return summed


def updated_link(fetcher, direction, coeffs):
    current = fetcher(direction, (0, 0, 0, 0))
    force = traceless_anti(matrix_product(current, staple_sum(fetcher, direction)))
    generator = -step_drift * force + step_noise * algebra(coeffs)
    return cayley(generator, current)


def extend(lattice, top_slice):
    stacked = jnp.concatenate([lattice, top_slice], axis=4)
    widened = extended_2(stacked, (("sx", 5),), 1)
    return extended_2(widened, (("syz", 6),), SITES_ALONG_Z)


def pick_field(extended, z_coord, x_count, yz_count, link_dir, offsets):
    t_step, x_step, y_step, z_step = offsets
    portion = extended[link_dir]
    if t_step == 1:
        portion = portion[:, :, :, 1:]
    else:
        portion = portion[:, :, :, :-1]
        if t_step == -1:
            portion = jnp.roll(portion, 1, axis=3)
    portion = portion[:, :, :, :, 1 + x_step : 1 + x_step + x_count]
    offset = (1 + y_step) * SITES_ALONG_Z
    portion = portion[:, :, :, :, :, offset : offset + yz_count]
    if z_step == 1:
        portion = jnp.where(
            z_coord == SITES_ALONG_Z - 1,
            jnp.roll(portion, SITES_ALONG_Z - 1, axis=-1),
            jnp.roll(portion, -1, axis=-1),
        )
    if z_step == -1:
        portion = jnp.where(
            z_coord == 0,
            jnp.roll(portion, 1 - SITES_ALONG_Z, axis=-1),
            jnp.roll(portion, 1, axis=-1),
        )
    return portion


def last_links(windows, gauge_links, langevin_noise):
    time_count, x_count, yz_count = gauge_links.shape[4:]
    y_count = yz_count // SITES_ALONG_Z
    time_coord = lax.axis_index("slab") * time_count + jnp.arange(time_count)
    x_coord = lax.axis_index("sx") * x_count + jnp.arange(x_count)
    cell_index = jnp.arange(yz_count)
    z_coord = cell_index % SITES_ALONG_Z
    yz_coord = lax.axis_index("syz") * y_count + cell_index // SITES_ALONG_Z + z_coord
    parity = (time_coord[:, None, None] + x_coord[None, :, None] + yz_coord[None, None, :]) % 2
    interior = jnp.broadcast_to((jnp.arange(time_count) != 0)[:, None, None], parity.shape)
    own = jnp.repeat(windows[:, :, :, :, OWN, 32:96], 2, axis=-1)
    lattice = gauge_links
    for (direction, time), index in FIELD_OF.items():
        if time < time_count:
            value = jnp.where(parity[time] == 0, own[index, 0], own[index, 1])
            lattice = lattice.at[direction, :, :, :, time].set(
                value.reshape(2, 3, 3, x_count, yz_count)
            )
    above_face = shifted(gauge_links[1:, :, :, :, 0:1], "slab", -1)
    top_slice = jnp.concatenate(
        [jnp.zeros_like(gauge_links[0:1, :, :, :, 0:1]), above_face], axis=0
    )
    for direction in range(1, 4):
        kick_field = langevin_noise[SWEEPS - 1, direction].astype(jnp.float32)
        for colour in range(2):
            extended = extend(lattice, top_slice)
            fetcher = partial(pick_field, extended, z_coord, x_count, yz_count)
            candidate = updated_link(fetcher, direction, kick_field)
            chosen = jnp.logical_and(parity == colour, interior)
            lattice = lattice.at[direction].set(
                jnp.where(chosen, candidate, lattice[direction])
            )
    return lattice


def local(gauge_links, langevin_noise, separations):
    def buffers(ends):
        halves = tuple(pltpu.VMEM((ends[1], 8, 128), jnp.float32) for _ in range(4))
        return (pltpu.VMEM((2 * ends[0], 8, 128), jnp.float32), *halves)

    sets = (FIRST_PAIRS, SECOND_PAIRS, LATE_PAIRS, TURN_PAIRS, TURN2_PAIRS)
    vmem = pl.BlockSpec(memory_space=pltpu.VMEM)
    links = jnp.swapaxes(gauge_links, 4, 5)
    kicks = jnp.swapaxes(langevin_noise, 3, 4)
    win_shape = (len(FIELDS), 2, 2, 9, 8, 128)
    correlator, windows = pl.pallas_call(
        kernel,
        out_shape=(
            jax.ShapeDtypeStruct((3, 1, 128), jnp.float32),
            jax.ShapeDtypeStruct(win_shape, jnp.float32),
        ),
        in_specs=[
            pl.BlockSpec(memory_space=pltpu.HBM),
            pl.BlockSpec(memory_space=pltpu.HBM),
            pl.BlockSpec(memory_space=pltpu.HBM),
        ],
        out_specs=(vmem, pl.BlockSpec(memory_space=pltpu.HBM)),
        scratch_shapes=[
            pltpu.VMEM(links.shape, jnp.float32),
            pltpu.VMEM(kicks.shape, kicks.dtype),
            pltpu.SMEM(separations.shape, jnp.int32),
            pltpu.SemaphoreType.DMA((4,)),
        ]
        + [buffers(pairs) for pairs in sets] + [
            pltpu.VMEM(win_shape, jnp.float32),
            pltpu.VMEM((len(KICKS), 2, 8, 8, 128), jnp.float32),
            pltpu.VMEM((4, 2, 3, 3, 8, 128), jnp.float32),
            pltpu.VMEM((SWEEPS, 4, 2 * LINK, 8, 128), jnp.float32),
            pltpu.SemaphoreType.DMA((COPIES,)),
            pltpu.SemaphoreType.DMA((COPIES,)),
        ],
        compiler_params=pltpu.CompilerParams(
            collective_id=0, has_side_effects=True, vmem_limit_bytes=VMEM_LIMIT
        ),
    )(links, kicks, separations)
    last_links(windows, gauge_links, langevin_noise)
    return jnp.swapaxes(correlator, 0, 1) * (1.0 / SWEEPS**4)


def solution(mesh):
    return jax.shard_map(
        local,
        mesh=mesh,
        in_specs=(
            P(None, None, None, None, "slab", "sx", "syz"),
            P(None, None, None, "slab", "sx", "syz"),
            P(),
        ),
        out_specs=P("slab", "sx", "syz"),
        check_vma=False,
    )
```

profile of v0, /device:TPU:1, one launch (start us, length us, event | category | flops | bytes accessed | tf_op | source)
XLA Modules:
  0.0 40.9 jit_solution(13650932248825593119)
XLA Ops:
  0.0 39.6 %shard_map.37 = (f32[3,1,128]{2,1,0:T(1,128)}, f32[11,2,2,9,8,128]{5,4,3,2,1,0:T(8,128)}) custom-call(f32[4,2,3,3,3,2,128]{6,5,4,3,2,1,0:T(2,128)} %bitcast.4, bf16[2,4,8,3,2,128]{5,4,3,2,1,0:T(2,128)(2,1)} %bitcast.5, s32[4]{0:T(128)} %separations_hbm.1), custom_call_target="tpu_custom_call" | custom-call | tf_op jit(solution)/shard_map/pallas_call | solution.py:888
  39.7 1.2 %multiply_bitcast_fusion = f32[1,3,128]{2,0,1:T(1,128)} fusion(f32[3,1,128]{2,1,0:T(1,128)} %get-tuple-element.6), kind=kLoop, calls=%fused_computation | loop fusion | flops 384 | bytes 3072 | tf_op jit(solution)/shard_map/mul | solution.py:919
where the time goes:
time: 41 us; the launch traced here: 40.9 us
  Pallas kernels  39.6 us (97%)
  other arithmetic  1.24 us (3%)
    pallas_call x1, Pallas kernels, local(): pl.pallas_call(kernel, out_shape=(jax.ShapeDtypeStruct((3, 1, 128), jnp.f...  39.6 us
    mul x1, other arithmetic, local(): return jnp.swapaxes(correlator, 0, 1) * (1.0 / SWEEPS ** 4)  1.24 us

commit v1 on v0

--- a/solution.py
+++ b/solution.py
@@ -15,7 +15,7 @@
 root_third = 0.5773502691896258
 
 MESH = pl.DeviceIdType.MESH
-VMEM_LIMIT = 60 * 1024 * 1024
+VMEM_LIMIT = 55168 * 1024
 
 OWN = slice(2, 5)
 FIELDS = ((0, 0), (0, 1), (1, 1), (2, 1), (3, 1), (1, 0), (2, 0), (3, 0), (1, 2), (2, 2), (3, 2))

time: 41 us -> 40.4 us (0.985)
  other arithmetic: 1.24 us -> 0.57 us
  local copies, waits for them, and re-layouts: 0 us -> 0.65 us
  Pallas kernels: 39.6 us -> 39 us
    mul x1, other arithmetic: 1.24 us -> 0.57 us  [local(): return jnp.swapaxes(correlator, 0, 1) * (1.0 / SWEEPS ** 4)]
    unnamed x0 -> x2, local copies, waits for them, and re-layouts: none -> 0.65 us
    pallas_call x1, Pallas kernels: 39.6 us -> 39 us  [local(): pl.pallas_call(kernel, out_shape=(jax.ShapeDtypeStruct((3, 1, 128), jnp.f...]
where the time goes in v1:
time: 40.4 us; the launch traced here: 40.3 us
  Pallas kernels  39 us (97%)
  local copies, waits for them, and re-layouts  0.65 us (2%)
  other arithmetic  0.57 us (1%)
    pallas_call x1, Pallas kernels, local(): pl.pallas_call(kernel, out_shape=(jax.ShapeDtypeStruct((3, 1, 128), jnp.f...  39 us

profile of v1, /device:TPU:1, one launch (start us, length us, event | category | flops | bytes accessed | tf_op | source)
XLA Modules:
  0.0 40.3 jit_solution(9475779059956172808)
XLA Ops:
  0.0 0.0 copy-start
  0.0 0.7 %copy-done = s32[4]{0:T(128)S(1)} copy-done((s32[4]{0:T(128)S(1)}, s32[4]{0:T(128)}, u32[]{:S(2)}) %copy-start) | copy-done | bytes 40
  0.7 39.0 %shard_map.37 = (f32[3,1,128]{2,1,0:T(1,128)S(1)}, f32[11,2,2,9,8,128]{5,4,3,2,1,0:T(8,128)}) custom-call(f32[4,2,3,3,3,2,128]{6,5,4,3,2,1,0:T(2,128)} %bitcast.4, bf16[2,4,8,3,2,128]{5,4,3,2,1,0:T(2,128)(2,1)} %bitcast.5, s32[4]{0:T(128)S(1)} %copy-done), custom_call_target="tpu_custom_call" | custom-call | tf_op jit(solution)/shard_map/pallas_call | solution.py:888
  39.7 0.6 %multiply_bitcast_fusion = f32[1,3,128]{2,0,1:T(1,128)} fusion(f32[3,1,128]{2,1,0:T(1,128)S(1)} %get-tuple-element.6), kind=kLoop, calls=%fused_computation | loop fusion | flops 384 | bytes 3072 | tf_op jit(solution)/shard_map/mul | solution.py:919
Async XLA Ops:
  0.0 0.7 %copy-start = (s32[4]{0:T(128)S(1)}, s32[4]{0:T(128)}, u32[]{:S(2)}) copy-start(s32[4]{0:T(128)} %separations_hbm.1) | copy-start | bytes 52
